TPU v7x, 32 devices: a whole 2x2x4 slice. The times are simulated.
32 devices in a mesh: gx: 4 (over z), gy: 2 (over y), gz: 4 (over x, core).
Axes of the slice: x: 2, y: 2, z: 4, core: 2. Of those that a mesh axis runs over, the one named last changes fastest.
Arguments:
- checkpoint: float32 [19, 64, 32, 512], P(None, 'gx', 'gy', 'gz'), may hold values from 0.005 to 0.6, as said below
- adjoint: float32 [19, 64, 32, 512], P(None, 'gx', 'gy', 'gz'), may hold values from -6 to 6
- porosity: float32 [64, 32, 512], P('gx', 'gy', 'gz'), may hold values from 0 to 0.5
- solid: int32 [64, 32, 512], P('gx', 'gy', 'gz'), may hold values 0 or 1
- gradient_in: float32 [64, 32, 512], P('gx', 'gy', 'gz'), may hold values from -6 to 6
Outputs:
- adjoint_out: float32 [19, 64, 32, 512], P(None, 'gx', 'gy', 'gz')
- gradient_out: float32 [64, 32, 512], P('gx', 'gy', 'gz')
Inputs may be any that keep to these rules, and one draw needn't show every extreme that they name: `checkpoint`: each population is positive and near w_i times a density of order one.
All inputs are finite; a program needn't handle non-finite values. No bound on the sum of `solid` on one device may be relied on, other than what follows from the above.
Results may differ from a plain program's by a relative error of at most 0.0001.
Values sent between devices are 32-bit elements; how exact they have to be, the bound alone decides.
A program may use at most 128 MiB of HBM per device.

v0:
```python
import functools

import jax
import jax.numpy as jnp
from jax import lax
from jax.experimental import pallas as pl
from jax.experimental.pallas import tpu as pltpu
from jax.sharding import PartitionSpec as P

RECOMP = 3
VELOCITIES = [
    (0, 0, 0),
    (1, 0, 0),
    (-1, 0, 0),
    (0, 1, 0),
    (0, -1, 0),
    (0, 0, 1),
    (0, 0, -1),
    (1, 1, 0),
    (-1, -1, 0),
    (1, -1, 0),
    (-1, 1, 0),
    (1, 0, 1),
    (-1, 0, -1),
    (1, 0, -1),
    (-1, 0, 1),
    (0, 1, 1),
    (0, -1, -1),
    (0, 1, -1),
    (0, -1, 1),
]
OPPOSITE = [0, 2, 1, 4, 3, 6, 5, 8, 7, 10, 9, 12, 11, 14, 13, 16, 15, 18, 17]
PAIRS = [(1, 2), (3, 4), (5, 6), (7, 8), (9, 10), (11, 12), (13, 14), (15, 16), (17, 18)]
WEIGHTS = [1.0 / 3.0] + [1.0 / 18.0] * 6 + [1.0 / 36.0] * 12
RELAX = 1.25

ORDER = [1, 7, 9, 11, 13, 2, 8, 10, 12, 14, 0, 3, 4, 5, 6, 15, 16, 17, 18]
SLOT = [ORDER.index(i) for i in range(19)]
Y_GROUP = [[i for i in range(19) if VELOCITIES[i][1] == s] for s in (1, -1)]
Z_GROUP = [[i for i in range(19) if VELOCITIES[i][2] == s] for s in (1, -1)]
AXES = ("gx", "gy", "gz")
ADJ = RECOMP
ROUNDS = RECOMP + 1
MESH_ID = pl.DeviceIdType.MESH


def side(component):
    return 0 if component > 0 else 1


def moments(f):
    plus = [f[i] + f[o] for i, o in PAIRS]
    minus = [f[i] - f[o] for i, o in PAIRS]
    rho = f[0]
    for s in plus:
        rho = rho + s
    flow = []
    for axis in range(3):
        total = None
        for (i, _), d in zip(PAIRS, minus):
            c = VELOCITIES[i][axis]
            if c == 0:
                continue
            total = d if total is None else (total + d if c > 0 else total - d)
        flow.append(total)
    return rho, flow


def along(vector, i):
    total = None
    for axis in range(3):
        c = VELOCITIES[i][axis]
        if c == 0:
            continue
        if total is None:
            total = vector[axis] if c > 0 else -vector[axis]
        else:
            total = total + vector[axis] if c > 0 else total - vector[axis]
    return total


def collide(f, gamma):
    rho, flow = moments(f)
    inv = 1.0 / rho
    u = [j * inv for j in flow]
    fluid = 1.0 - gamma
    keep = (1.0 - RELAX) * fluid
    gain = RELAX * fluid
    scaled = gain * rho
    squared = u[0] * u[0] + u[1] * u[1] + u[2] * u[2]
    base = scaled - 1.5 * scaled * squared
    triple = (3.0 / 36.0) * scaled
    base_edge = (1.0 / 36.0) * base
    base_face = base_edge + base_edge
    post = [None] * 19
    post[0] = (keep + gamma) * f[0] + (1.0 / 3.0) * base
    for i, o in PAIRS:
        q = along(u, i)
        t = triple * q
        even = 1.5 * q * t
        if i < 7:
            t = t + t
            even = even + even + base_face
        else:
            even = even + base_edge
        post[i] = keep * f[i] + gamma * f[o] + (even + t)
        post[o] = keep * f[o] + gamma * f[i] + (even - t)
    return post


def kernel(nx, ny, nz, chunk, ck_hbm, adj_hbm, por_hbm, sol_hbm, gin_hbm, out_hbm, grad_hbm,
           ck, post, ystage, yhalo, zstage, zrecv, zmerge, base, coef, gsum, por, sol, gin,
           outv, gradv, send_sem, recv_sem, ck_sem, adj_sem, small_sem, out_sem):
    sizes = [lax.axis_size(a) for a in AXES]
    me = [lax.axis_index(a) for a in AXES]
    chunks = nx // chunk

    def device(i):
        return tuple(
            lax.rem(m + v + n, n) if v else m for m, v, n in zip(me, VELOCITIES[i], sizes)
        )

    barrier = pltpu.get_barrier_semaphore()
    for i in range(1, 19):
        pl.semaphore_signal(barrier, inc=1, device_id=device(i), device_id_type=MESH_ID)

    def ck_copy(c):
        span = pl.ds(c * chunk, chunk)
        return pltpu.make_async_copy(ck_hbm.at[:, span], ck.at[:, span], ck_sem.at[c])

    def adj_copy(j):
        return pltpu.make_async_copy(
            adj_hbm.at[j], post.at[ADJ, SLOT[OPPOSITE[j]], pl.ds(1, nx)], adj_sem.at[j]
        )

    smalls = [
        pltpu.make_async_copy(por_hbm, por, small_sem.at[0]),
        pltpu.make_async_copy(sol_hbm, sol, small_sem.at[1]),
        pltpu.make_async_copy(gin_hbm, gin, small_sem.at[2]),
    ]
    smalls[0].start()
    smalls[1].start()
    for c in range(chunks):
        ck_copy(c).start()
    for j in range(19):
        adj_copy(j).start()
    smalls[2].start()

    def message(r, i):
        ex, ey, ez = VELOCITIES[i]
        if ez:
            d = side(ez)
            src, dst = zstage.at[r, d], zrecv.at[r, d, Z_GROUP[d].index(i)]
        elif ey and ex:
            d = side(ey)
            k = Y_GROUP[d].index(i)
            src = ystage.at[r, d, k, nx - 1 if ex > 0 else 0]
            dst = yhalo.at[r, d, k, 0 if ex > 0 else nx + 1]
        elif ey:
            d = side(ey)
            src, dst = ystage.at[r, d], yhalo.at[r, d, :, pl.ds(1, nx)]
        else:
            group = pl.ds(5 * side(ex), 5)
            src = post.at[r, group, nx if ex > 0 else 1]
            dst = post.at[r, group, 0 if ex > 0 else nx + 1]
        return pltpu.make_async_remote_copy(
            src_ref=src, dst_ref=dst, send_sem=send_sem.at[r, i], recv_sem=recv_sem.at[r, i],
            device_id=device(i), device_id_type=MESH_ID,
        )

    lane = lax.broadcasted_iota(jnp.int32, (ny, nz), 1)
    row = lax.broadcasted_iota(jnp.int32, (ny, nz), 0)
    lane_in = lax.rem(lane, nx)

    def stage(r, x, v, packed):
        result = []
        for d in range(2):
            edge = ny - 1 if d == 0 else 0
            for k, i in enumerate(Y_GROUP[d]):
                ystage[r, d, k, x] = v(i)[edge : edge + 1]
            total = None
            for k, i in enumerate(Z_GROUP[d]):
                turn = (k * nx + (1 if d == 0 else 0)) % nz
                moved = pltpu.roll(v(i), turn, 1) if turn else v(i)
                total = moved if total is None else jnp.where(lane < k * nx, total, moved)
            total = pltpu.roll(total, x, 1)
            result.append(jnp.where(lane_in == x, total, packed[d]))
        return tuple(result)

    def send(r, packed):
        for d in range(2):
            zstage[r, d] = packed[d]
        for i in range(1, 19):
            message(r, i).start()

    def receive(r):
        for i in range(1, 19):
            message(r, i).wait_recv()
        for d in range(2):
            face = zrecv[r, d, 0]
            merged = face
            for k, i in enumerate(Z_GROUP[d]):
                if k == 0:
                    continue
                ex, ey, _ = VELOCITIES[i]
                other = zrecv[r, d, k]
                if ex > 0:
                    part = jnp.where(
                        lane_in == 0, pltpu.roll(other, nz - (nx - 1), 1), pltpu.roll(face, 1, 1)
                    )
                elif ex < 0:
                    part = jnp.where(
                        lane_in == nx - 1, pltpu.roll(other, nx - 1, 1), pltpu.roll(face, nz - 1, 1)
                    )
                elif ey > 0:
                    part = jnp.where(row == 0, pltpu.roll(other, 1, 0), pltpu.roll(face, 1, 0))
                else:
                    part = jnp.where(
                        row == ny - 1, pltpu.roll(other, ny - 1, 0), pltpu.roll(face, ny - 1, 0)
                    )
                merged = jnp.where(lane // nx == k, part, merged)
            zmerge[r, d] = merged

    def streamed(r, x):
        turned = [pltpu.roll(zmerge[r, d], lax.rem(nz - x, nz), 1) for d in range(2)]
        f = []
        for i in range(19):
            ex, ey, ez = VELOCITIES[i]
            v = post[r, SLOT[i], x + 1 - ex]
            if ey:
                d = side(ey)
                halo = yhalo[r, d, Y_GROUP[d].index(i), x + 1 - ex]
                v = jnp.where(
                    row == (0 if ey > 0 else ny - 1),
                    jnp.broadcast_to(halo, (ny, nz)),
                    pltpu.roll(v, 1 if ey > 0 else ny - 1, 0),
                )
            if ez:
                d = side(ez)
                k = Z_GROUP[d].index(i)
                target = 0 if ez > 0 else nz - 1
                turn = (target - k * nx) % nz
                halo = pltpu.roll(turned[d], turn, 1) if turn else turned[d]
                v = jnp.where(
                    lane == target, halo, pltpu.roll(v, 1 if ez > 0 else nz - 1, 1)
                )
            f.append(v)
        return f

    def gamma_at(x):
        return jnp.where(sol[x] == 1, 1.0, por[x])

    zero = jnp.zeros((ny, nz), jnp.float32)

    def forward(r, f, x, packed):
        out = collide(f, gamma_at(x))
        for i in range(19):
            post[r, SLOT[i], x + 1] = out[i]
        return stage(r, x, lambda i: out[i], packed)

    smalls[0].wait()
    smalls[1].wait()

    def first(c, packed):
        ck_copy(c).wait()

        def plane(x, packed):
            return forward(0, [ck[i, x] for i in range(19)], x, packed)

        return lax.fori_loop(c * chunk, (c + 1) * chunk, plane, packed)

    packed = lax.fori_loop(0, chunks, first, (zero, zero))
    pl.semaphore_wait(barrier, 18)
    send(0, packed)

    for j in range(19):
        adj_copy(j).wait()
    packed = lax.fori_loop(
        0, nx, lambda x, p: stage(ADJ, x, lambda i: post[ADJ, SLOT[i], x + 1], p), (zero, zero)
    )
    send(ADJ, packed)

    for r in range(1, RECOMP):
        receive(r - 1)
        packed = lax.fori_loop(
            0, nx, lambda x, p, r=r: forward(r, streamed(r - 1, x), x, p), (zero, zero)
        )
        send(r, packed)

    receive(ADJ)

    def pull(x, carry):
        h = streamed(ADJ, x)
        g = [h[OPPOSITE[i]] for i in range(19)]
        gamma = gamma_at(x)
        keep = (1.0 - RELAX) * (1.0 - gamma)
        w = [WEIGHTS[0] * g[0]] + [None] * 18
        g0 = WEIGHTS[0] * g[0]
        g1 = [None] * 3
        g2 = {}
        base[0, x] = (keep + gamma) * g[0]
        coef[0, x] = RELAX * g[0]
        for i, o in PAIRS:
            plus = WEIGHTS[i] * (g[i] + g[o])
            minus = WEIGHTS[i] * (g[i] - g[o])
            g0 = g0 + plus
            v = VELOCITIES[i]
            for a in range(3):
                if v[a]:
                    term = minus if v[a] > 0 else -minus
                    g1[a] = term if g1[a] is None else g1[a] + term
                for b in range(a, 3):
                    if v[a] * v[b]:
                        term = plus if v[a] * v[b] > 0 else -plus
                        g2[a, b] = term if (a, b) not in g2 else g2[a, b] + term
            base[i, x] = keep * g[i] + gamma * g[o]
            base[o, x] = keep * g[o] + gamma * g[i]
            coef[i, x] = g[o] + (RELAX - 1.0) * g[i]
            coef[o, x] = g[i] + (RELAX - 1.0) * g[o]
        gsum[0, x] = g0
        for a in range(3):
            gsum[1 + a, x] = g1[a]
        for n, key in enumerate([(0, 0), (1, 1), (2, 2), (0, 1), (0, 2), (1, 2)]):
            gsum[4 + n, x] = g2[key]
        return carry

    lax.fori_loop(0, nx, pull, 0)
    smalls[2].wait()
    last = RECOMP - 1
    receive(last)

    def out_copy(c):
        span = pl.ds(c * chunk, chunk)
        return pltpu.make_async_copy(outv.at[:, span], out_hbm.at[:, span], out_sem.at[c])

    def final(x, carry):
        f = streamed(last, x)
        rho, flow = moments(f)
        inv = 1.0 / rho
        u = [j * inv for j in flow]
        g0 = gsum[0, x]
        g1 = [gsum[1 + a, x] for a in range(3)]
        xx, yy, zz, xy, xz, yz = [gsum[4 + n, x] for n in range(6)]
        gu = [
            xx * u[0] + xy * u[1] + xz * u[2],
            xy * u[0] + yy * u[1] + yz * u[2],
            xz * u[0] + yz * u[1] + zz * u[2],
        ]
        squared = u[0] * u[0] + u[1] * u[1] + u[2] * u[2]
        quad = 4.5 * (u[0] * gu[0] + u[1] * gu[1] + u[2] * gu[2]) - 1.5 * g0 * squared
        gain = RELAX * (1.0 - gamma_at(x))
        slope = gain * (g0 - quad)
        vec = [gain * (3.0 * g1[a] + 9.0 * gu[a] - 3.0 * g0 * u[a]) for a in range(3)]
        total = f[0] * coef[0, x]
        for i in range(1, 19):
            total = total + f[i] * coef[i, x]
        g1j = g1[0] * flow[0] + g1[1] * flow[1] + g1[2] * flow[2]
        total = total - RELAX * (rho * (g0 + quad) + 3.0 * g1j)
        pore = 1.0 - sol[x].astype(jnp.float32)
        gradv[x] = gin[x] + pore * total
        outv[0, x] = base[0, x] + slope
        for i, o in PAIRS:
            q = along(vec, i)
            outv[i, x] = base[i, x] + (slope + q)
            outv[o, x] = base[o, x] + (slope - q)
        return carry

    def finish(c, carry):
        lax.fori_loop(c * chunk, (c + 1) * chunk, final, 0)
        out_copy(c).start()
        return carry

    lax.fori_loop(0, chunks, finish, 0)
    grad_copy = pltpu.make_async_copy(gradv, grad_hbm, small_sem.at[3])
    grad_copy.start()
    for r in range(ROUNDS):
        for i in range(1, 19):
            message(r, i).wait_send()
    for c in range(chunks):
        out_copy(c).wait()
    grad_copy.wait()


def body(checkpoint, adjoint, porosity, solid, gradient_in):
    _, nx, ny, nz = checkpoint.shape
    chunk = 4 if nx % 4 == 0 else 1
    chunks = nx // chunk
    f32 = jnp.float32
    block = (nx, ny, nz)
    vm = pltpu.VMEM
    dma = pltpu.SemaphoreType.DMA
    return pl.pallas_call(
        functools.partial(kernel, nx, ny, nz, chunk),
        out_shape=(
            jax.ShapeDtypeStruct((19,) + block, f32),
            jax.ShapeDtypeStruct(block, f32),
        ),
        in_specs=[pl.BlockSpec(memory_space=pl.ANY)] * 5,
        out_specs=(pl.BlockSpec(memory_space=pl.ANY),) * 2,
        scratch_shapes=[
            vm((19,) + block, f32),
            vm((ROUNDS, 19, nx + 2, ny, nz), f32),
            vm((ROUNDS, 2, 5, nx, 1, nz), f32),
            vm((ROUNDS, 2, 5, nx + 2, 1, nz), f32),
            vm((ROUNDS, 2, ny, nz), f32),
            vm((ROUNDS, 2, 5, ny, nz), f32),
            vm((ROUNDS, 2, ny, nz), f32),
            vm((19,) + block, f32),
            vm((19,) + block, f32),
            vm((10,) + block, f32),
            vm(block, f32),
            vm(block, jnp.int32),
            vm(block, f32),
            vm((19,) + block, f32),
            vm(block, f32),
            dma((ROUNDS, 19)),
            dma((ROUNDS, 19)),
            dma((chunks,)),
            dma((19,)),
            dma((4,)),
            dma((chunks,)),
        ],
        compiler_params=pltpu.CompilerParams(
            collective_id=0, has_side_effects=True, vmem_limit_bytes=48 * 1024 * 1024
        ),
    )(checkpoint, adjoint, porosity, solid, gradient_in)


def solution(mesh):
    in_specs = (
        P(None, "gx", "gy", "gz"),
        P(None, "gx", "gy", "gz"),
        P("gx", "gy", "gz"),
        P("gx", "gy", "gz"),
        P("gx", "gy", "gz"),
    )
    out_specs = (P(None, "gx", "gy", "gz"), P("gx", "gy", "gz"))
    return jax.shard_map(body, mesh=mesh, in_specs=in_specs, out_specs=out_specs, check_vma=False)
```

profile of v0, /device:TPU:0, one launch (start us, length us, event | category | flops | bytes accessed | tf_op | source)
XLA Modules:
  0.0 47.6 jit_solution(5140737872600692242)
XLA Ops:
  0.6 0.0 copy-start
  0.6 1.7 %copy-done = f32[19,16,16,128]{3,2,1,0:T(8,128)S(1)} copy-done((f32[19,16,16,128]{3,2,1,0:T(8,128)S(1)}, f32[19,16,16,128]{3,2,1,0:T(8,128)}, u32[]{:S(2)}) %copy-start) | copy-done | bytes 2490392
  2.3 0.0 copy-start.1
  2.3 0.9 %copy-done.1 = f32[16,16,128]{2,1,0:T(8,128)S(1)} copy-done((f32[16,16,128]{2,1,0:T(8,128)S(1)}, f32[16,16,128]{2,1,0:T(8,128)}, u32[]{:S(2)}) %copy-start.1) | copy-done | bytes 131096
  3.2 0.0 copy-start.2
  3.2 0.9 %copy-done.2 = s32[16,16,128]{2,1,0:T(8,128)S(1)} copy-done((s32[16,16,128]{2,1,0:T(8,128)S(1)}, s32[16,16,128]{2,1,0:T(8,128)}, u32[]{:S(2)}) %copy-start.2) | copy-done | bytes 131096
  4.1 0.0 copy-start.3
  4.1 0.9 %copy-done.3 = f32[16,16,128]{2,1,0:T(8,128)S(1)} copy-done((f32[16,16,128]{2,1,0:T(8,128)S(1)}, f32[16,16,128]{2,1,0:T(8,128)}, u32[]{:S(2)}) %copy-start.3) | copy-done | bytes 131096
  5.0 40.5 %shard_map.68 = (f32[19,16,16,128]{3,2,1,0:T(8,128)S(1)}, f32[16,16,128]{2,1,0:T(8,128)S(1)}) custom-call(f32[19,16,16,128]{3,2,1,0:T(8,128)S(1)} %copy-done, f32[19,16,16,128]{3,2,1,0:T(8,128)} %adj_hbm.1, f32[16,16,128]{2,1,0:T(8,128)S(1)} %copy-done.1, s32[16,16,128]{2,1,0:T(8,128)S(1)} %copy-done.2, f32[16,16,128]{2,1,0:T(8,128)S(1)} %copy-done.3), custom_call_target="tpu_custom_call" | custom-call | tf_op jit(solution)/shard_map/pallas_call | solution.py:392
  45.5 1.5 %copy.9 = f32[19,16,16,128]{3,2,1,0:T(8,128)} copy(f32[19,16,16,128]{3,2,1,0:T(8,128)S(1)} %get-tuple-element.4) | data formatting | bytes 4980736
  47.0 0.7 %copy.10 = f32[16,16,128]{2,1,0:T(8,128)} copy(f32[16,16,128]{2,1,0:T(8,128)S(1)} %get-tuple-element.5) | data formatting | bytes 262144
Async XLA Ops:
  0.6 1.7 %copy-start = (f32[19,16,16,128]{3,2,1,0:T(8,128)S(1)}, f32[19,16,16,128]{3,2,1,0:T(8,128)}, u32[]{:S(2)}) copy-start(f32[19,16,16,128]{3,2,1,0:T(8,128)} %ck_hbm.1) | copy-start | bytes 7471108
  2.3 0.9 %copy-start.1 = (f32[16,16,128]{2,1,0:T(8,128)S(1)}, f32[16,16,128]{2,1,0:T(8,128)}, u32[]{:S(2)}) copy-start(f32[16,16,128]{2,1,0:T(8,128)} %por_hbm.1) | copy-start | bytes 393220
  3.2 0.9 %copy-start.2 = (s32[16,16,128]{2,1,0:T(8,128)S(1)}, s32[16,16,128]{2,1,0:T(8,128)}, u32[]{:S(2)}) copy-start(s32[16,16,128]{2,1,0:T(8,128)} %sol_hbm.1) | copy-start | bytes 393220
  4.1 0.9 %copy-start.3 = (f32[16,16,128]{2,1,0:T(8,128)S(1)}, f32[16,16,128]{2,1,0:T(8,128)}, u32[]{:S(2)}) copy-start(f32[16,16,128]{2,1,0:T(8,128)} %gin_hbm.1) | copy-start | bytes 393220
where the time goes:
time: 47.8 us; the launch traced here: 47.6 us
  Pallas kernels  40.5 us (85%)
  local copies, waits for them, and re-layouts  6.51 us (14%)
  between operations  0.65 us (1%)
    pallas_call x1, Pallas kernels, body(): pl.pallas_call(functools.partial(kernel, nx, ny, nz, chunk), out_shape=(j...  40.5 us
    unnamed x10, local copies, waits for them, and re-layouts  6.51 us

commit v1 on v0

--- a/solution.py
+++ b/solution.py
@@ -108,9 +108,9 @@
     return post
 
 
-def kernel(nx, ny, nz, chunk, ck_hbm, adj_hbm, por_hbm, sol_hbm, gin_hbm, out_hbm, grad_hbm,
-           ck, post, ystage, yhalo, zstage, zrecv, zmerge, base, coef, gsum, por, sol, gin,
-           outv, gradv, send_sem, recv_sem, ck_sem, adj_sem, small_sem, out_sem):
+def kernel(nx, ny, nz, chunk, ck_hbm, adj_hbm, por_hbm, sol_hbm, gin_hbm, outv, gradv,
+           ck, post, ystage, yhalo, zstage, zrecv, base, coef, gsum, por, sol, gin,
+           send_sem, recv_sem, ck_sem, adj_sem, small_sem):
     sizes = [lax.axis_size(a) for a in AXES]
     me = [lax.axis_index(a) for a in AXES]
     chunks = nx // chunk
@@ -142,9 +142,6 @@
     smalls[1].start()
     for c in range(chunks):
         ck_copy(c).start()
-    for j in range(19):
-        adj_copy(j).start()
-    smalls[2].start()
 
     def message(r, i):
         ex, ey, ez = VELOCITIES[i]
@@ -170,21 +167,24 @@
 
     lane = lax.broadcasted_iota(jnp.int32, (ny, nz), 1)
     row = lax.broadcasted_iota(jnp.int32, (ny, nz), 0)
-    lane_in = lax.rem(lane, nx)
+
+    def turned(i, x, v):
+        ez = VELOCITIES[i][2]
+        if ez == 0:
+            return v
+        k = Z_GROUP[side(ez)].index(i) * nx + x
+        return pltpu.roll(v, k + 1 if ez > 0 else k, 1)
 
     def stage(r, x, v, packed):
         result = []
         for d in range(2):
             edge = ny - 1 if d == 0 else 0
             for k, i in enumerate(Y_GROUP[d]):
-                ystage[r, d, k, x] = v(i)[edge : edge + 1]
-            total = None
+                ystage[r, d, k, x] = v[i][edge : edge + 1]
+            total = packed[d]
             for k, i in enumerate(Z_GROUP[d]):
-                turn = (k * nx + (1 if d == 0 else 0)) % nz
-                moved = pltpu.roll(v(i), turn, 1) if turn else v(i)
-                total = moved if total is None else jnp.where(lane < k * nx, total, moved)
-            total = pltpu.roll(total, x, 1)
-            result.append(jnp.where(lane_in == x, total, packed[d]))
+                total = jnp.where(lane == k * nx + x, v[i], total)
+            result.append(total)
         return tuple(result)
 
     def send(r, packed):
@@ -196,54 +196,32 @@
     def receive(r):
         for i in range(1, 19):
             message(r, i).wait_recv()
-        for d in range(2):
-            face = zrecv[r, d, 0]
-            merged = face
-            for k, i in enumerate(Z_GROUP[d]):
-                if k == 0:
-                    continue
-                ex, ey, _ = VELOCITIES[i]
-                other = zrecv[r, d, k]
-                if ex > 0:
-                    part = jnp.where(
-                        lane_in == 0, pltpu.roll(other, nz - (nx - 1), 1), pltpu.roll(face, 1, 1)
-                    )
-                elif ex < 0:
-                    part = jnp.where(
-                        lane_in == nx - 1, pltpu.roll(other, nx - 1, 1), pltpu.roll(face, nz - 1, 1)
-                    )
-                elif ey > 0:
-                    part = jnp.where(row == 0, pltpu.roll(other, 1, 0), pltpu.roll(face, 1, 0))
-                else:
-                    part = jnp.where(
-                        row == ny - 1, pltpu.roll(other, ny - 1, 0), pltpu.roll(face, ny - 1, 0)
-                    )
-                merged = jnp.where(lane // nx == k, part, merged)
-            zmerge[r, d] = merged
 
     def streamed(r, x):
-        turned = [pltpu.roll(zmerge[r, d], lax.rem(nz - x, nz), 1) for d in range(2)]
         f = []
         for i in range(19):
             ex, ey, ez = VELOCITIES[i]
             v = post[r, SLOT[i], x + 1 - ex]
+            if ez:
+                d = side(ez)
+                n = Z_GROUP[d].index(i)
+                at = lax.rem(x - ex + nx, nx) if ex else x
+                k = n * nx + at
+                outer = (nx - x) // nx if ex > 0 else (x + 1) // nx if ex < 0 else 0
+                v = jnp.where(lane == k, zrecv[r, d, n * outer], v)
             if ey:
-                d = side(ey)
-                halo = yhalo[r, d, Y_GROUP[d].index(i), x + 1 - ex]
+                e = side(ey)
+                halo = yhalo[r, e, Y_GROUP[e].index(i), x + 1 - ex]
+                if ez:
+                    edge = ny - 1 if ey > 0 else 0
+                    halo = jnp.where(lane[:1] == k, zrecv[r, d, n, edge : edge + 1], halo)
                 v = jnp.where(
                     row == (0 if ey > 0 else ny - 1),
                     jnp.broadcast_to(halo, (ny, nz)),
                     pltpu.roll(v, 1 if ey > 0 else ny - 1, 0),
                 )
             if ez:
-                d = side(ez)
-                k = Z_GROUP[d].index(i)
-                target = 0 if ez > 0 else nz - 1
-                turn = (target - k * nx) % nz
-                halo = pltpu.roll(turned[d], turn, 1) if turn else turned[d]
-                v = jnp.where(
-                    lane == target, halo, pltpu.roll(v, 1 if ez > 0 else nz - 1, 1)
-                )
+                v = pltpu.roll(v, lax.rem(nz - k, nz) if ez > 0 else nz - 1 - k, 1)
             f.append(v)
         return f
 
@@ -253,10 +231,16 @@
     zero = jnp.zeros((ny, nz), jnp.float32)
 
     def forward(r, f, x, packed):
-        out = collide(f, gamma_at(x))
+        out = [turned(i, x, v) for i, v in enumerate(collide(f, gamma_at(x)))]
         for i in range(19):
             post[r, SLOT[i], x + 1] = out[i]
-        return stage(r, x, lambda i: out[i], packed)
+        return stage(r, x, out, packed)
+
+    def lift(x, packed):
+        out = [turned(i, x, post[ADJ, SLOT[i], x + 1]) for i in range(19)]
+        for i in Z_GROUP[0] + Z_GROUP[1]:
+            post[ADJ, SLOT[i], x + 1] = out[i]
+        return stage(ADJ, x, out, packed)
 
     smalls[0].wait()
     smalls[1].wait()
@@ -269,21 +253,23 @@
 
         return lax.fori_loop(c * chunk, (c + 1) * chunk, plane, packed)
 
-    packed = lax.fori_loop(0, chunks, first, (zero, zero))
+    packed = lax.fori_loop(0, chunks // 2, first, (zero, zero))
+    for j in range(19):
+        adj_copy(j).start()
+    smalls[2].start()
+    packed = lax.fori_loop(chunks // 2, chunks, first, packed)
     pl.semaphore_wait(barrier, 18)
     send(0, packed)
 
     for j in range(19):
         adj_copy(j).wait()
-    packed = lax.fori_loop(
-        0, nx, lambda x, p: stage(ADJ, x, lambda i: post[ADJ, SLOT[i], x + 1], p), (zero, zero)
-    )
+    packed = lax.fori_loop(0, nx, lift, (zero, zero), unroll=4)
     send(ADJ, packed)
 
     for r in range(1, RECOMP):
         receive(r - 1)
         packed = lax.fori_loop(
-            0, nx, lambda x, p, r=r: forward(r, streamed(r - 1, x), x, p), (zero, zero)
+            0, nx, lambda x, p, r=r: forward(r, streamed(r - 1, x), x, p), (zero, zero), unroll=4
         )
         send(r, packed)
 
@@ -324,14 +310,10 @@
             gsum[4 + n, x] = g2[key]
         return carry
 
-    lax.fori_loop(0, nx, pull, 0)
+    lax.fori_loop(0, nx, pull, 0, unroll=4)
     smalls[2].wait()
     last = RECOMP - 1
     receive(last)
-
-    def out_copy(c):
-        span = pl.ds(c * chunk, chunk)
-        return pltpu.make_async_copy(outv.at[:, span], out_hbm.at[:, span], out_sem.at[c])
 
     def final(x, carry):
         f = streamed(last, x)
@@ -365,20 +347,10 @@
             outv[o, x] = base[o, x] + (slope - q)
         return carry
 
-    def finish(c, carry):
-        lax.fori_loop(c * chunk, (c + 1) * chunk, final, 0)
-        out_copy(c).start()
-        return carry
-
-    lax.fori_loop(0, chunks, finish, 0)
-    grad_copy = pltpu.make_async_copy(gradv, grad_hbm, small_sem.at[3])
-    grad_copy.start()
+    lax.fori_loop(0, nx, final, 0, unroll=4)
     for r in range(ROUNDS):
         for i in range(1, 19):
             message(r, i).wait_send()
-    for c in range(chunks):
-        out_copy(c).wait()
-    grad_copy.wait()
 
 
 def body(checkpoint, adjoint, porosity, solid, gradient_in):
@@ -395,8 +367,8 @@
             jax.ShapeDtypeStruct((19,) + block, f32),
             jax.ShapeDtypeStruct(block, f32),
         ),
-        in_specs=[pl.BlockSpec(memory_space=pl.ANY)] * 5,
-        out_specs=(pl.BlockSpec(memory_space=pl.ANY),) * 2,
+        in_specs=[pl.BlockSpec(memory_space=pltpu.HBM)] * 5,
+        out_specs=(pl.BlockSpec(memory_space=pltpu.VMEM),) * 2,
         scratch_shapes=[
             vm((19,) + block, f32),
             vm((ROUNDS, 19, nx + 2, ny, nz), f32),
@@ -404,24 +376,20 @@
             vm((ROUNDS, 2, 5, nx + 2, 1, nz), f32),
             vm((ROUNDS, 2, ny, nz), f32),
             vm((ROUNDS, 2, 5, ny, nz), f32),
-            vm((ROUNDS, 2, ny, nz), f32),
             vm((19,) + block, f32),
             vm((19,) + block, f32),
             vm((10,) + block, f32),
             vm(block, f32),
             vm(block, jnp.int32),
             vm(block, f32),
-            vm((19,) + block, f32),
-            vm(block, f32),
             dma((ROUNDS, 19)),
             dma((ROUNDS, 19)),
             dma((chunks,)),
             dma((19,)),
-            dma((4,)),
-            dma((chunks,)),
+            dma((3,)),
         ],
         compiler_params=pltpu.CompilerParams(
-            collective_id=0, has_side_effects=True, vmem_limit_bytes=48 * 1024 * 1024
+            collective_id=0, has_side_effects=True, vmem_limit_bytes=62 * 1024 * 1024
         ),
     )(checkpoint, adjoint, porosity, solid, gradient_in)
 

time: 47.8 us -> 37.7 us (0.79)
  Pallas kernels: 40.5 us -> 32.8 us
  local copies, waits for them, and re-layouts: 6.51 us -> 4.06 us
    pallas_call x1, Pallas kernels: 40.5 us -> 32.8 us  [body(): pl.pallas_call(functools.partial(kernel, nx, ny, nz, chunk), out_shape=(j...]
    unnamed x10 -> x4, local copies, waits for them, and re-layouts: 6.51 us -> 4.06 us
where the time goes in v1:
time: 37.7 us; the launch traced here: 37.5 us
  Pallas kernels  32.8 us (87%)
  local copies, waits for them, and re-layouts  4.06 us (11%)
  between operations  0.65 us (2%)
    pallas_call x1, Pallas kernels, body(): pl.pallas_call(functools.partial(kernel, nx, ny, nz, chunk), out_shape=(j...  32.8 us
    unnamed x4, local copies, waits for them, and re-layouts  4.06 us

profile of v1, /device:TPU:0, one launch (start us, length us, event | category | flops | bytes accessed | tf_op | source)
XLA Modules:
  0.0 37.5 jit_solution(17007778668857248470)
XLA Ops:
  0.6 32.8 %shard_map.68 = (f32[19,16,16,128]{3,2,1,0:T(8,128)}, f32[16,16,128]{2,1,0:T(8,128)}) custom-call(f32[19,16,16,128]{3,2,1,0:T(8,128)} %ck_hbm.1, f32[19,16,16,128]{3,2,1,0:T(8,128)} %adj_hbm.1, f32[16,16,128]{2,1,0:T(8,128)} %por_hbm.1, s32[16,16,128]{2,1,0:T(8,128)} %sol_hbm.1, f32[16,16,128]{2,1,0:T(8,128)} %gin_hbm.1), custom_call_target="tpu_custom_call" | custom-call | tf_op jit(solution)/shard_map/pallas_call | solution.py:364
  33.5 0.0 copy-start
  33.5 3.4 %copy.9 = f32[19,16,16,128]{3,2,1,0:T(8,128)} copy(f32[19,16,16,128]{3,2,1,0:T(8,128)} %get-tuple-element.4) | data formatting | bytes 4980736
  36.9 0.0 copy-done
  36.9 0.7 %copy.10 = f32[16,16,128]{2,1,0:T(8,128)} copy(f32[16,16,128]{2,1,0:T(8,128)S(1)} %copy-done) | data formatting | bytes 262144
Async XLA Ops:
  33.5 3.4 %copy-start = (f32[16,16,128]{2,1,0:T(8,128)S(1)}, f32[16,16,128]{2,1,0:T(8,128)}, u32[]{:S(2)}) copy-start(f32[16,16,128]{2,1,0:T(8,128)} %get-tuple-element.5) | copy-start | bytes 393220

commit v2 on v1

--- a/solution.py
+++ b/solution.py
@@ -38,6 +38,8 @@
 SLOT = [ORDER.index(i) for i in range(19)]
 Y_GROUP = [[i for i in range(19) if VELOCITIES[i][1] == s] for s in (1, -1)]
 Z_GROUP = [[i for i in range(19) if VELOCITIES[i][2] == s] for s in (1, -1)]
+X_MESSAGES = [i for i in range(1, 19) if VELOCITIES[i][0]]
+REST_MESSAGES = [i for i in range(1, 19) if not VELOCITIES[i][0]]
 AXES = ("gx", "gy", "gz")
 ADJ = RECOMP
 ROUNDS = RECOMP + 1
@@ -108,12 +110,11 @@
     return post
 
 
-def kernel(nx, ny, nz, chunk, ck_hbm, adj_hbm, por_hbm, sol_hbm, gin_hbm, outv, gradv,
-           ck, post, ystage, yhalo, zstage, zrecv, base, coef, gsum, por, sol, gin,
+def kernel(nx, ny, nz, ck_hbm, adj_hbm, por_hbm, sol_hbm, gin_hbm, outv, gradv,
+           ck, post, ystage, yhalo, zstage, zedge, zrecv, base, coef, gsum, por, sol, gin,
            send_sem, recv_sem, ck_sem, adj_sem, small_sem):
     sizes = [lax.axis_size(a) for a in AXES]
     me = [lax.axis_index(a) for a in AXES]
-    chunks = nx // chunk
 
     def device(i):
         return tuple(
@@ -124,8 +125,11 @@
     for i in range(1, 19):
         pl.semaphore_signal(barrier, inc=1, device_id=device(i), device_id_type=MESH_ID)
 
+    half = nx // 2
+    spans = [(0, 1), (nx - 1, 1), (1, half - 1), (half, nx - 1 - half)]
+
     def ck_copy(c):
-        span = pl.ds(c * chunk, chunk)
+        span = pl.ds(*spans[c])
         return pltpu.make_async_copy(ck_hbm.at[:, span], ck.at[:, span], ck_sem.at[c])
 
     def adj_copy(j):
@@ -140,14 +144,15 @@
     ]
     smalls[0].start()
     smalls[1].start()
-    for c in range(chunks):
+    for c in range(4):
         ck_copy(c).start()
 
     def message(r, i):
         ex, ey, ez = VELOCITIES[i]
         if ez:
             d = side(ez)
-            src, dst = zstage.at[r, d], zrecv.at[r, d, Z_GROUP[d].index(i)]
+            src = zedge.at[r, d] if ex else zstage.at[r, d]
+            dst = zrecv.at[r, d, Z_GROUP[d].index(i)]
         elif ey and ex:
             d = side(ey)
             k = Y_GROUP[d].index(i)
@@ -187,10 +192,16 @@
             result.append(total)
         return tuple(result)
 
-    def send(r, packed):
+    def send_x(r, packed):
+        for d in range(2):
+            zedge[r, d] = packed[d]
+        for i in X_MESSAGES:
+            message(r, i).start()
+
+    def send_rest(r, packed):
         for d in range(2):
             zstage[r, d] = packed[d]
-        for i in range(1, 19):
+        for i in REST_MESSAGES:
             message(r, i).start()
 
     def receive(r):
@@ -245,33 +256,43 @@
     smalls[0].wait()
     smalls[1].wait()
 
-    def first(c, packed):
-        ck_copy(c).wait()
-
-        def plane(x, packed):
-            return forward(0, [ck[i, x] for i in range(19)], x, packed)
-
-        return lax.fori_loop(c * chunk, (c + 1) * chunk, plane, packed)
-
-    packed = lax.fori_loop(0, chunks // 2, first, (zero, zero))
+    def first(x, packed):
+        return forward(0, [ck[i, x] for i in range(19)], x, packed)
+
+    def edge_planes(step, packed):
+        return lax.fori_loop(0, 2, lambda n, p: step(n * (nx - 1), p), packed, unroll=2)
+
+    ck_copy(0).wait()
+    ck_copy(1).wait()
+    packed = edge_planes(first, (zero, zero))
+    edge_packed = packed
+    ck_copy(2).wait()
     for j in range(19):
         adj_copy(j).start()
     smalls[2].start()
-    packed = lax.fori_loop(chunks // 2, chunks, first, packed)
+    packed = lax.fori_loop(1, half, first, packed)
     pl.semaphore_wait(barrier, 18)
-    send(0, packed)
+    send_x(0, edge_packed)
+    ck_copy(3).wait()
+    packed = lax.fori_loop(half, nx - 1, first, packed)
+    send_rest(0, packed)
 
     for j in range(19):
         adj_copy(j).wait()
     packed = lax.fori_loop(0, nx, lift, (zero, zero), unroll=4)
-    send(ADJ, packed)
+    send_x(ADJ, packed)
+    send_rest(ADJ, packed)
 
     for r in range(1, RECOMP):
         receive(r - 1)
-        packed = lax.fori_loop(
-            0, nx, lambda x, p, r=r: forward(r, streamed(r - 1, x), x, p), (zero, zero), unroll=4
-        )
-        send(r, packed)
+
+        def step(x, p, r=r):
+            return forward(r, streamed(r - 1, x), x, p)
+
+        packed = edge_planes(step, (zero, zero))
+        send_x(r, packed)
+        packed = lax.fori_loop(1, nx - 1, step, packed, unroll=7)
+        send_rest(r, packed)
 
     receive(ADJ)
 
@@ -355,14 +376,12 @@
 
 def body(checkpoint, adjoint, porosity, solid, gradient_in):
     _, nx, ny, nz = checkpoint.shape
-    chunk = 4 if nx % 4 == 0 else 1
-    chunks = nx // chunk
     f32 = jnp.float32
     block = (nx, ny, nz)
     vm = pltpu.VMEM
     dma = pltpu.SemaphoreType.DMA
     return pl.pallas_call(
-        functools.partial(kernel, nx, ny, nz, chunk),
+        functools.partial(kernel, nx, ny, nz),
         out_shape=(
             jax.ShapeDtypeStruct((19,) + block, f32),
             jax.ShapeDtypeStruct(block, f32),
@@ -375,6 +394,7 @@
             vm((ROUNDS, 2, 5, nx, 1, nz), f32),
             vm((ROUNDS, 2, 5, nx + 2, 1, nz), f32),
             vm((ROUNDS, 2, ny, nz), f32),
+            vm((ROUNDS, 2, ny, nz), f32),
             vm((ROUNDS, 2, 5, ny, nz), f32),
             vm((19,) + block, f32),
             vm((19,) + block, f32),
@@ -384,7 +404,7 @@
             vm(block, f32),
             dma((ROUNDS, 19)),
             dma((ROUNDS, 19)),
-            dma((chunks,)),
+            dma((4,)),
             dma((19,)),
             dma((3,)),
         ],

time: 37.7 us -> 34.5 us (0.915)
  Pallas kernels: 32.8 us -> 29.6 us
    pallas_call x1, Pallas kernels: 32.8 us -> 29.6 us  [body(): pl.pallas_call(functools.partial(kernel, nx, ny, nz), out_shape=(jax.Shap...]
where the time goes in v2:
time: 34.5 us; the launch traced here: 34.3 us
  Pallas kernels  29.6 us (86%)
  local copies, waits for them, and re-layouts  4.06 us (12%)
  between operations  0.65 us (2%)
    pallas_call x1, Pallas kernels, body(): pl.pallas_call(functools.partial(kernel, nx, ny, nz), out_shape=(jax.Shap...  29.6 us
    unnamed x4, local copies, waits for them, and re-layouts  4.06 us

profile of v2, /device:TPU:0, one launch (start us, length us, event | category | flops | bytes accessed | tf_op | source)
XLA Modules:
  0.0 34.3 jit_solution(10792091671038435123)
XLA Ops:
  0.6 29.6 %shard_map.68 = (f32[19,16,16,128]{3,2,1,0:T(8,128)}, f32[16,16,128]{2,1,0:T(8,128)}) custom-call(f32[19,16,16,128]{3,2,1,0:T(8,128)} %ck_hbm.1, f32[19,16,16,128]{3,2,1,0:T(8,128)} %adj_hbm.1, f32[16,16,128]{2,1,0:T(8,128)} %por_hbm.1, s32[16,16,128]{2,1,0:T(8,128)} %sol_hbm.1, f32[16,16,128]{2,1,0:T(8,128)} %gin_hbm.1), custom_call_target="tpu_custom_call" | custom-call | tf_op jit(solution)/shard_map/pallas_call | solution.py:383
  30.2 0.0 copy-start
  30.2 3.4 %copy.9 = f32[19,16,16,128]{3,2,1,0:T(8,128)} copy(f32[19,16,16,128]{3,2,1,0:T(8,128)} %get-tuple-element.4) | data formatting | bytes 4980736
  33.6 0.0 copy-done
  33.6 0.7 %copy.10 = f32[16,16,128]{2,1,0:T(8,128)} copy(f32[16,16,128]{2,1,0:T(8,128)S(1)} %copy-done) | data formatting | bytes 262144
Async XLA Ops:
  30.2 3.4 %copy-start = (f32[16,16,128]{2,1,0:T(8,128)S(1)}, f32[16,16,128]{2,1,0:T(8,128)}, u32[]{:S(2)}) copy-start(f32[16,16,128]{2,1,0:T(8,128)} %get-tuple-element.5) | copy-start | bytes 393220
